TPU v7x, 32 devices: a whole 2x2x4 slice. The times are simulated.
32 devices in a mesh: shard: 16 (over z, y, x), rep: 2 (over core).
Axes of the slice: x: 2, y: 2, z: 4, core: 2. Of those that a mesh axis runs over, the one named last changes fastest.
Arguments:
- queries_in: bfloat16 [4096, 2560], P(('shard', 'rep')), may hold values from -6 to 6
- keys_in: bfloat16 [4096, 2560], P(('shard', 'rep')), may hold values from -6 to 6
- values_in: bfloat16 [4096, 2560], P(('shard', 'rep')), may hold values from -6 to 6
- gate_z: bfloat16 [4096, 2560], P(('shard', 'rep')), may hold values from -6 to 6
- beta_logit: bfloat16 [4096, 20], P(('shard', 'rep')), may hold values from -6 to 6
- decay_in: bfloat16 [4096, 20], P(('shard', 'rep')), may hold values from -6 to 6
- a_log: float32 [20], replicated, may hold values from -4.5 to 0.5
- dt_bias: float32 [20], replicated, may hold values from -2 to 1
- conv_weight: float32 [3, 4, 2560], replicated, may hold values from -3 to 3
- norm_gain: float32 [128], replicated, may hold values from 0.1 to 1.9
- out_weight: bfloat16 [2560, 2560], P('shard'), may hold values from -0.125 to 0.125
- out_grad: bfloat16 [4096, 2560], P(('shard', 'rep')), may hold values from -6 to 6
Outputs:
- layer_out: bfloat16 [4096, 2560], P(('shard', 'rep'))
- grad_queries: bfloat16 [4096, 2560], P(('shard', 'rep'))
- grad_keys: bfloat16 [4096, 2560], P(('shard', 'rep'))
- grad_values: bfloat16 [4096, 2560], P(('shard', 'rep'))
- grad_gate: bfloat16 [4096, 2560], P(('shard', 'rep'))
- grad_beta: bfloat16 [4096, 20], P(('shard', 'rep'))
- grad_decay: bfloat16 [4096, 20], P(('shard', 'rep'))
- grad_conv: float32 [3, 4, 2560], replicated
- grad_alog: float32 [20], replicated
- grad_bias: float32 [20], replicated
- grad_gain: float32 [128], replicated
- grad_out_weight: float32 [2560, 2560], P('shard')
All inputs are finite; a program needn't handle non-finite values.
Results may differ from a plain program's by a relative error of at most 0.012.
Values may be sent and summed in bfloat16 or wider, within the bound.
A program may use at most 256 MiB of HBM per device.

v0:
```python
import jax
import jax.numpy as jnp
from jax import lax
from jax.sharding import PartitionSpec as P

HEADS = 20
DK = 128
GROUP = 64


def causal_conv(signal, kernel):
    extent = kernel.shape[0]
    length = signal.shape[0]
    padded = jnp.pad(signal, ((extent - 1, 0), (0, 0)))
    summed = kernel[0] * padded[0:length]
    for offset in range(1, extent):
        summed = summed + kernel[offset] * padded[offset : offset + length]
    return jax.nn.silu(summed)


def unit_heads(field):
    shaped = field.reshape(field.shape[0], HEADS, DK)
    return shaped * lax.rsqrt(jnp.sum(shaped * shaped, axis=-1, keepdims=True) + 1e-06)


def prepare(queries_in, keys_in, values_in, beta_logit, decay_in, conv_weight, a_log, dt_bias):
    queries = unit_heads(causal_conv(queries_in.astype(jnp.float32), conv_weight[0])) * DK ** (-0.5)
    keys = unit_heads(causal_conv(keys_in.astype(jnp.float32), conv_weight[1]))
    values = causal_conv(values_in.astype(jnp.float32), conv_weight[2]).reshape(
        values_in.shape[0], HEADS, DK
    )
    betas = jax.nn.sigmoid(beta_logit.astype(jnp.float32))
    decays = -jnp.exp(a_log) * jax.nn.softplus(decay_in.astype(jnp.float32) + dt_bias)
    return (queries, keys, values, betas, decays)


def finish(mixed, gate_z, norm_gain):
    normed = mixed * lax.rsqrt(jnp.mean(mixed * mixed, axis=-1, keepdims=True) + 1e-06) * norm_gain
    gates = jax.nn.silu(gate_z.astype(jnp.float32)).reshape(gate_z.shape[0], HEADS, DK)
    return (normed * gates).reshape(gate_z.shape[0], HEADS * DK)


def blockwise(queries, keys, values, betas, decays):
    length = queries.shape[0]
    blocks = length // GROUP
    exact = lax.Precision.HIGHEST

    def arrange(field):
        return field.reshape(blocks, GROUP, HEADS, DK).transpose(0, 2, 1, 3)

    def arrange_small(field):
        return field.reshape(blocks, GROUP, HEADS).transpose(0, 2, 1)

    lower = jnp.tril(jnp.ones((GROUP, GROUP), jnp.float32))
    identity = jnp.eye(GROUP, dtype=jnp.float32)
    strict = lower - identity

    def advance(state, inputs):
        query, key, value, beta, decay = inputs
        cumul = jnp.einsum("hj,ij->hi", decay, lower, precision=exact)
        spread = cumul[:, :, None] - cumul[:, None, :]
        weights = jnp.exp(jnp.where(lower > 0, spread, 0.0)) * lower
        key_dots = jnp.einsum("hik,hjk->hij", key, key, precision=exact)
        system = identity + beta[:, :, None] * weights * key_dots * strict
        scale_in = jnp.exp(cumul)[:, :, None]
        rhs_side = beta[:, :, None] * (
            value - scale_in * jnp.einsum("hvk,hik->hiv", state, key, precision=exact)
        )
        corrected = jax.scipy.linalg.solve_triangular(
            system, rhs_side, lower=True, unit_diagonal=True
        )
        query_dots = jnp.einsum("hik,hjk->hij", query, key, precision=exact)
        mixed = scale_in * jnp.einsum("hvk,hik->hiv", state, query, precision=exact)
        mixed = mixed + jnp.einsum("hij,hjv->hiv", weights * query_dots, corrected, precision=exact)
        tail_decay = jnp.exp(cumul[:, -1:] - cumul)
        state = jnp.exp(cumul[:, -1])[:, None, None] * state
        state = state + jnp.einsum(
            "hjv,hjk->hvk", tail_decay[:, :, None] * corrected, key, precision=exact
        )
        return (state, mixed)

    start = jnp.zeros((HEADS, DK, DK), jnp.float32)
    _, mixed = lax.scan(
        advance,
        start,
        (
            arrange(queries),
            arrange(keys),
            arrange(values),
            arrange_small(betas),
            arrange_small(decays),
        ),
    )
    return mixed.transpose(0, 2, 1, 3).reshape(length, HEADS, DK)


def mixer(
    queries_in,
    keys_in,
    values_in,
    gate_z,
    beta_logit,
    decay_in,
    conv_weight,
    a_log,
    dt_bias,
    norm_gain,
):
    queries, keys, values, betas, decays = prepare(
        queries_in, keys_in, values_in, beta_logit, decay_in, conv_weight, a_log, dt_bias
    )
    return finish(blockwise(queries, keys, values, betas, decays), gate_z, norm_gain)


def shards(
    queries_in,
    keys_in,
    values_in,
    gate_z,
    beta_logit,
    decay_in,
    a_log,
    dt_bias,
    conv_weight,
    norm_gain,
    out_weight,
    out_grad,
):
    hidden_f, pullback = jax.vjp(
        mixer,
        queries_in,
        keys_in,
        values_in,
        gate_z,
        beta_logit,
        decay_in,
        conv_weight,
        a_log,
        dt_bias,
        norm_gain,
    )
    hidden = hidden_f.astype(jnp.bfloat16)
    back_dims = (((1,), (1,)), ((), ()))
    gathered = lax.all_gather(out_weight, "shard", axis=0, tiled=True)
    layer_out = jnp.dot(hidden, gathered, preferred_element_type=jnp.float32).astype(jnp.bfloat16)
    grad_hidden = lax.dot_general(
        out_grad, gathered, back_dims, preferred_element_type=jnp.float32
    ).astype(jnp.bfloat16)
    grads = pullback(grad_hidden.astype(jnp.float32))
    own_part = lax.psum_scatter(
        lax.dot_general(
            hidden, out_grad, (((0,), (0,)), ((), ())), preferred_element_type=jnp.float32
        ),
        "shard",
        scatter_dimension=0,
        tiled=True,
    )
    grad_out_weight = lax.psum(own_part, "rep")
    grad_conv, grad_alog, grad_bias, grad_gain = lax.psum(
        (grads[6], grads[7], grads[8], grads[9]), ("shard", "rep")
    )
    return (
        layer_out,
        grads[0],
        grads[1],
        grads[2],
        grads[3],
        grads[4],
        grads[5],
        grad_conv,
        grad_alog,
        grad_bias,
        grad_gain,
        grad_out_weight,
    )


def solution(mesh):
    placed = (
        P(("shard", "rep"), None),
        P(("shard", "rep"), None),
        P(("shard", "rep"), None),
        P(("shard", "rep"), None),
        P(("shard", "rep"), None),
        P(("shard", "rep"), None),
        P(),
        P(),
        P(),
        P(),
        P("shard", None),
        P(("shard", "rep"), None),
    )
    return jax.shard_map(
        shards,
        mesh=mesh,
        in_specs=placed,
        out_specs=(
            P(("shard", "rep"), None),
            P(("shard", "rep"), None),
            P(("shard", "rep"), None),
            P(("shard", "rep"), None),
            P(("shard", "rep"), None),
            P(("shard", "rep"), None),
            P(("shard", "rep"), None),
            P(),
            P(),
            P(),
            P(),
            P("shard", None),
        ),
        check_vma=False,
    )
```

profile of v0, /device:TPU:0, one launch (start us, length us, event | category | flops | bytes accessed | tf_op | source)
XLA Modules:
  0.0 1038.8 jit_solution(14371931021873199466)
XLA Ops:
  17.7 2.9 fusion.235
  20.7 2.6 reshape.520
  23.3 2.9 copy.135
  30.1 2.5 reshape.519
  32.6 2.8 copy.139
  36.4 2.9 fusion.234
  46.7 254.7 %while.84 = (s32[]{:T(128)}, f32[20,128,128]{2,1,0:T(8,128)S(1)}, f32[2,20,64,128]{3,2,1,0:T(8,128)}, f32[2,20,64,64]{3,2,1,0:T(8,128)}, f32[2,20,64,64]{3,2,1,0...) while((s32[]{:T(128)}, f32[20,128,128]{2,1,0:T(8,128)S(1)}, ...), condition=%wide.region_3.4_spmd.clone.clone, body=%wide.region_2.3_spmd.clone.clone.sunk | while | flops 1264813312 | bytes 103854688 | solution.py:83
  48.8 3.7 bitcast_dynamic-update-slice_fusion.32
  53.6 3.5 bitcast_dynamic-update-slice_fusion.30
  60.3 99.7 %custom-call.42 = f32[20,1,64,64]{2,3,1,0:T(8,128)} custom-call(f32[20,1,64,64]{3,2,1,0:T(8,128)} %add_bitcast_fusion.8), custom_call_target="InvertDiagBlocksLowerTriangular" | custom-call | tf_op jit(solution)/shard_map/jvp()/while/body/eval_jaxpr/jit(_solve_triangular)/vmap()/triangular_solve | solution.py:69
  160.0 4.4 bitcast_dynamic-update-slice_fusion.31
  164.3 2.6 convolution_add_fusion.15
  175.6 3.7 bitcast_dynamic-update-slice_fusion.32
  180.5 3.5 bitcast_dynamic-update-slice_fusion.30
  187.2 99.7 %custom-call.42 = f32[20,1,64,64]{2,3,1,0:T(8,128)} custom-call(f32[20,1,64,64]{3,2,1,0:T(8,128)} %add_bitcast_fusion.8), custom_call_target="InvertDiagBlocksLowerTriangular" | custom-call | tf_op jit(solution)/shard_map/jvp()/while/body/eval_jaxpr/jit(_solve_triangular)/vmap()/triangular_solve | solution.py:69
  286.9 4.3 bitcast_dynamic-update-slice_fusion.31
  291.2 2.6 convolution_add_fusion.15
  301.4 3.3 copy.140
  307.2 11.5 %fusion.222 = (bf16[128,2560]{1,0:T(8,128)(2,1)}, bf16[128,2560]{1,0:T(8,128)(2,1)S(1)}, f32[128,2560]{1,0:T(8,128)}) fusion(bf16[128,2560]{1,0:T(8,128)(2,1)} %param.19, f32[2560]{0:T(1024)S(1)} %broadcast_bitcast_fusion, f32[128,2560]{1,0:T(8,128)} %copy.142, f32[16,8,20,128]{3,2,1,0:T(8,128)} %bitcast.540, bf16[128,2560]{1,0:T(8,128)(2,1)S(1)} %copy-done, ...), kind=kOutput, calls=%fused_computation.287 | convolution fusion | flops 1684275200 | bytes 19671040 | tf_op jit(solution)/shard_map/dot_general | solution.py:146
  318.7 10.6 %fusion.253 = f32[2560,2560]{1,0:T(8,128)} fusion(bf16[128,2560]{1,0:T(8,128)(2,1)S(1)} %get-tuple-element.1871, bf16[128,2560]{1,0:T(8,128)(2,1)S(1)} %copy-done), kind=kOutput, calls=%fused_computation.413 | convolution fusion | flops 1677721600 | bytes 27525120 | tf_op jit(solution)/shard_map/dot_general | solution.py:151
  331.1 2.8 copy.155
  333.9 2.5 mul.1127
  336.4 4.0 fusion.214
  347.0 271.6 %while.83 = (s32[]{:T(128)}, f32[20,128,128]{2,1,0:T(8,128)S(1)}, f32[2,20,64,128]{3,2,1,0:T(8,128)}, f32[2,20,64,128]{3,2,1,0:T(8,128)}, f32[2,20,64,128]{3,2,1...) while((s32[]{:T(128)}, f32[20,128,128]{2,1,0:T(8,128)S(1)}, ...), condition=%wide.region_16.17_spmd.clone, body=%wide.region_6.16_spmd.clone.sunk | while | flops 2589384192 | bytes 154396208 | solution.py:83
  349.6 2.8 fusion.334
  357.5 99.7 %custom-call.41 = f32[20,1,64,64]{2,3,1,0:T(8,128)} custom-call(f32[20,1,64,64]{3,2,1,0:T(8,128)} %add_bitcast_fusion.7), custom_call_target="InvertDiagBlocksLowerTriangular" | custom-call | tf_op jit(solution)/shard_map/transpose(jvp())/while/body/eval_jaxpr/jit(_solve_triangular)/vmap()/triangular_solve | solution.py:69
  457.2 2.6 fusion.338
  459.8 3.3 fusion.339
  466.5 2.6 convolution_add_fusion.11
  470.0 2.6 convolution_add_fusion.13
  485.1 2.8 fusion.334
  493.0 99.7 %custom-call.41 = f32[20,1,64,64]{2,3,1,0:T(8,128)} custom-call(f32[20,1,64,64]{3,2,1,0:T(8,128)} %add_bitcast_fusion.7), custom_call_target="InvertDiagBlocksLowerTriangular" | custom-call | tf_op jit(solution)/shard_map/transpose(jvp())/while/body/eval_jaxpr/jit(_solve_triangular)/vmap()/triangular_solve | solution.py:69
  592.7 2.6 fusion.338
  595.3 3.3 fusion.339
  602.1 2.6 convolution_add_fusion.11
  605.5 2.6 convolution_add_fusion.13
  630.1 2.9 copy.156
  640.9 5.3 multiply_reduce_fusion.2
  651.8 3.9 broadcast_multiply_fusion.1
  657.9 2.5 broadcast_multiply_fusion.5
  660.6 3.9 fusion.232
  664.5 56.1 %all-reduce.32 = (f32[20]{0:T(128)}, f32[20]{0:T(128)}, f32[128]{0:T(128)}) all-reduce(f32[20]{0:T(128)S(1)} %negate_multiply_fusion, f32[20]{0:T(128)S(1)} %get-tuple-element.1822, f32[128]{0:T(128)S(1)} %copy-done.121), channel_id=1, replica_groups=mesh['shard'=16,'rep'=2] {'shard','rep'}, use_global_device_ids=true, to_apply=%region_33.34 | all-reduce | flops 168 | bytes 1344 | tf_op jit(solution)/shard_map/psum | solution.py:159
  720.7 151.2 %reduce-scatter.2.cloned.1.call-done = f32[160,2560]{1,0:T(8,128)} async-done(((f32[2560,2560]{1,0:T(8,128)}), f32[160,2560]{1,0:T(8,128)}) %reduce-scatter.2.cloned.1.call-update) | async-done | bytes 1638416 | tf_op jit(solution)/shard_map/reduce_scatter | solution.py:150
  872.5 3.2 fusion.231
  877.2 7.4 convolution_convert_fusion.1
  884.6 120.3 %all-reduce.36.cloned.1.call-done = f32[3,4,2560]{2,1,0:T(4,128)} async-done(((f32[3,4,2560]{2,1,0:T(4,128)}), f32[3,4,2560]{2,1,0:T(4,128)}) %all-reduce.36.cloned.1.call-update) | async-done | bytes 122896 | tf_op jit(solution)/shard_map/psum | solution.py:159
  1004.9 22.9 %all-reduce.38.cloned.1.call-done = f32[160,2560]{1,0:T(8,128)} async-done(((f32[160,2560]{1,0:T(8,128)}), f32[160,2560]{1,0:T(8,128)}) %all-reduce.38.cloned.1.call-update) | async-done | bytes 1638416 | tf_op jit(solution)/shard_map/psum | solution.py:158
  1029.4 2.7 copy.336
  (556 shorter events, 132.7 us)
Async XLA Ops:
  7.2 300.0 %copy-start = (bf16[128,2560]{1,0:T(8,128)(2,1)S(1)}, bf16[128,2560]{1,0:T(8,128)(2,1)}, u32[]{:S(2)}) copy-start(bf16[128,2560]{1,0:T(8,128)(2,1)} %param.27) | copy-start | bytes 1966084
  7.2 300.0 %all-gather.2.cloned.1.call-start = ((), (), s32[]{:S(2)}) async-start(), calls=%async_computation.1 | async-start | bytes 13926400 | tf_op jit(solution)/shard_map/all_gather | solution.py:144
  7.9 863.9 %reduce-scatter.2.cloned.1.call-start = ((), (), s32[]{:S(2)}) async-start(), calls=%async_computation.3 | async-start | bytes 27852800 | tf_op jit(solution)/shard_map/reduce_scatter | solution.py:150
  9.7 7.9 copy-start.93
  9.7 7.9 copy-start.95
  9.7 7.9 copy-start.97
  9.7 7.9 copy-start.99
  9.8 7.9 copy-start.101
  9.8 7.9 copy-start.103
  9.8 7.9 copy-start.104
  9.8 7.9 copy-start.105
  15.8 10.9 %copy-start.35 = (f32[128,2560]{0,1:T(8,128)}, f32[128,2560]{0,1:T(8,128)S(1)}, u32[]{:S(2)}) copy-start(f32[128,2560]{0,1:T(8,128)S(1)} %copy.133) | copy-start | bytes 3932164
  47.0 6.6 copy-start.29
  48.8 4.8 copy-start.18
  48.8 4.8 copy-start.26
  160.0 6.9 copy-start.23
  160.0 7.0 copy-start.52
  160.0 7.0 copy-start.55
  173.9 6.6 copy-start.29
  175.6 4.8 copy-start.18
  175.6 4.8 copy-start.26
  286.9 6.9 copy-start.23
  286.9 6.9 copy-start.52
  286.9 6.9 copy-start.55
  318.7 10.6 %copy-start.59 = (bf16[128,2560]{1,0:T(8,128)(2,1)}, bf16[128,2560]{1,0:T(8,128)(2,1)S(1)}, u32[]{:S(2)}) copy-start(bf16[128,2560]{1,0:T(8,128)(2,1)S(1)} %get-tuple-element.1871) | copy-start | bytes 1966084
  329.3 675.6 %all-reduce.36.cloned.1.call-start = ((), (), s32[]{:S(2)}) async-start(), calls=%async_computation.2 | async-start | bytes 245760 | tf_op jit(solution)/shard_map/psum | solution.py:159
  336.4 4.1 copy-start.22
  336.4 4.1 copy-start.34
  349.6 3.5 copy-start.2
  349.6 3.5 copy-start.57
  640.9 5.4 copy-start.47
  640.9 5.4 copy-start.58
  640.9 5.4 copy-start.69
  640.9 5.4 copy-start.70
  640.9 5.4 copy-start.71
  640.9 5.4 copy-start.75
  651.8 4.0 copy-start.73
  651.8 4.0 copy-start.86
  651.8 4.0 copy-start.88
  651.8 4.0 copy-start.90
  651.8 4.0 copy-start.92
  660.5 367.3 %all-reduce.38.cloned.1.call-start = ((), (), s32[]{:S(2)}) async-start(), calls=%async_computation.4 | async-start | bytes 3276800 | tf_op jit(solution)/shard_map/psum | solution.py:158
  660.5 3.9 copy-start.123
  660.5 3.9 copy-start.121
  660.6 60.0 %copy-start.107 = (f32[2,20,64]{2,1,0:T(8,128)S(1)}, f32[2,20,64]{2,1,0:T(8,128)}, u32[]{:S(2)}) copy-start(f32[2,20,64]{2,1,0:T(8,128)} %copy-done.106) | copy-start | bytes 30724
  664.4 207.4 %copy-start.114 = (bf16[128,20]{0,1:T(8,128)(2,1)S(1)}, bf16[128,20]{0,1:T(8,128)(2,1)}, u32[]{:S(2)}) copy-start(bf16[128,20]{0,1:T(8,128)(2,1)} %param.20) | copy-start | bytes 15364
  664.4 208.1 %copy-start.64 = (f32[128,2560]{1,0:T(8,128)S(1)}, f32[128,2560]{1,0:T(8,128)}, u32[]{:S(2)}) copy-start(f32[128,2560]{1,0:T(8,128)} %get-tuple-element.1878) | copy-start | bytes 3932164
  1027.8 4.3 copy-start.1
  (123 other events, 266.6 us)
Sparse Core Ops, SparseCore 0:
  10.8 160.7 all-gather.1
  329.4 542.4 reduce-scatter.1
  878.0 126.8 all-reduce.35
  1007.1 20.6 all-reduce.37
where the time goes:
time: 1050 us; the launch traced here: 1040 us
  other arithmetic  463 us (44%)
  waiting for transfers between devices  295 us (28%)
  matrix products  120 us (11%)
  local copies, waits for them, and re-layouts  86.3 us (8%)
  blocking collectives  56.1 us (5%)
  between operations  15.2 us (1%)
    another operation x18, other arithmetic, advance(): jax.scipy.linalg.solve_triangular(system, rhs_side, lower=True, unit_diag...  403 us
    reduce_scatter x1, waiting for transfers between devices, shards(): lax.psum_scatter(lax.dot_general(hidden, out_grad, (((0,), (0,)), ((), ()...  151 us
    psum x1, waiting for transfers between devices, shards(): lax.psum((grads[6], grads[7], grads[8], grads[9]), ('shard', 'rep'))  120 us
    psum x1, blocking collectives, shards(): lax.psum((grads[6], grads[7], grads[8], grads[9]), ('shard', 'rep'))  56.1 us
    psum x1, waiting for transfers between devices, shards(): grad_out_weight = lax.psum(own_part, 'rep')  22.9 us
  transfers between devices with their start and end apart: 4, of which 3 were waited for; matrix products, arithmetic and copies ran while one was open for 60% of the time, Pallas kernels for 0%

commit v1 on v0

v1 whole, which is shorter than its diff:
```python
import functools

import jax
import jax.numpy as jnp
from jax import lax
from jax.experimental import pallas as pl
from jax.experimental.pallas import tpu as pltpu
from jax.sharding import PartitionSpec as P

DK = 128
STEP_HEADS = 4
EPS = 1e-06
F32 = jnp.float32
BF16 = jnp.bfloat16


def split(x):
    high = x.astype(BF16)
    return high, (x - high.astype(F32)).astype(BF16)


def mm(a, b):
    left = jnp.concatenate([a[0], a[0], a[1]], axis=1)
    right = jnp.concatenate([b[0], b[1], b[0]], axis=0)
    return jnp.dot(left, right, preferred_element_type=F32)


def mm_t(a, b):
    left = jnp.concatenate([a[0], a[0], a[1]], axis=1)
    right = jnp.concatenate([b[0], b[1], b[0]], axis=1)
    return lax.dot_general(left, right, (((1,), (1,)), ((), ())), preferred_element_type=F32)


def shift_down(x, count):
    if count == 0:
        return x
    rows = lax.broadcasted_iota(jnp.int32, x.shape, 0)
    return jnp.where(rows >= count, pltpu.roll(x, count, 0), 0.0)


def shift_up(x, count):
    if count == 0:
        return x
    rows = lax.broadcasted_iota(jnp.int32, x.shape, 0)
    size = x.shape[0]
    return jnp.where(rows < size - count, pltpu.roll(x, size - count, 0), 0.0)


def conv(x, w):
    taps = w.shape[0]
    total = w[0:1] * shift_down(x, taps - 1)
    for j in range(1, taps):
        total = total + w[j : j + 1] * shift_down(x, taps - 1 - j)
    return total


def sigmoid(x):
    return 1.0 / (1.0 + jnp.exp(-x))


def softplus(x):
    return jnp.maximum(x, 0.0) + jnp.log1p(jnp.exp(-jnp.abs(x)))


def grids(size):
    rows = lax.broadcasted_iota(jnp.int32, (size, size), 0)
    cols = lax.broadcasted_iota(jnp.int32, (size, size), 1)
    return rows, cols


def invert(system, rows, cols):
    size = system.shape[0]
    eye = (rows == cols).astype(F32)

    def corner(block):
        keep = (rows // (2 * block) == cols // (2 * block)) & (rows // block > cols // block)
        return jnp.where(keep, system, 0.0)

    inverse = eye - corner(1)
    block = 2
    while block < size:
        parts = split(inverse)
        inverse = inverse - mm(parts, split(mm(split(corner(block)), parts)))
        block *= 2
    return inverse


def gates(beta_ref, decay_ref, alog_ref, bias_ref):
    beta = sigmoid(beta_ref[...].astype(F32))
    logit = decay_ref[...].astype(F32) + bias_ref[...]
    decay = -jnp.exp(alog_ref[...]) * softplus(logit)
    return beta, logit, decay


def running(decay, rows, cols):
    lower = (rows >= cols).astype(F32)
    return jnp.dot(lower, decay, precision=lax.Precision.HIGHEST, preferred_element_type=F32)


def column(field, head):
    lanes = lax.broadcasted_iota(jnp.int32, field.shape, 1)
    return jnp.sum(jnp.where(lanes == head, field, 0.0), axis=1, keepdims=True)


def forward(xq, xk, xv, wq, wk, wv, beta, total, rows, cols):
    pq, pk, pv = conv(xq, wq), conv(xk, wk), conv(xv, wv)
    sq, sk, sv = sigmoid(pq), sigmoid(pk), sigmoid(pv)
    yq, yk, value = pq * sq, pk * sk, pv * sv
    rq = lax.rsqrt(jnp.sum(yq * yq, axis=1, keepdims=True) + EPS)
    rk = lax.rsqrt(jnp.sum(yk * yk, axis=1, keepdims=True) + EPS)
    query, key = yq * rq, yk * rk
    query_s, key_s = split(query * DK**-0.5), split(key)
    total_row = jnp.sum(jnp.where(rows == cols, total, 0.0), axis=0, keepdims=True)
    lower = rows >= cols
    weights = jnp.where(lower, jnp.exp(jnp.where(lower, total - total_row, 0.0)), 0.0)
    key_dots = mm_t(key_s, key_s)
    query_dots = mm_t(query_s, key_s)
    strict = jnp.where(rows > cols, weights, 0.0)
    inverse = invert(beta * strict * key_dots, rows, cols)
    corrected = mm(split(inverse), split(beta * value))
    mixing = weights * query_dots
    mixed = mm(split(mixing), split(corrected))
    return mixed, (
        (pq, pk, pv), (sq, sk, sv), value, (rq, rk), (query, key), (query_s, key_s),
        weights, strict, key_dots, mixing, inverse, corrected,
    )


def hidden_kernel(
    q_ref, k_ref, v_ref, z_ref, beta_ref, decay_ref, alog_ref, bias_ref, conv_ref, gain_ref, out_ref
):
    size = q_ref.shape[0]
    rows, cols = grids(size)
    betas, _, decay = gates(beta_ref, decay_ref, alog_ref, bias_ref)
    totals = running(decay, rows, cols)
    first = pl.program_id(0) * STEP_HEADS
    for i in range(STEP_HEADS):
        at = slice(i * DK, (i + 1) * DK)
        mixed, _ = forward(
            q_ref[:, at].astype(F32), k_ref[:, at].astype(F32), v_ref[:, at].astype(F32),
            conv_ref[0, :, at], conv_ref[1, :, at], conv_ref[2, :, at],
            column(betas, first + i), column(totals, first + i), rows, cols,
        )
        z = z_ref[:, at].astype(F32)
        r = lax.rsqrt(jnp.mean(mixed * mixed, axis=1, keepdims=True) + EPS)
        out_ref[:, at] = (mixed * r * gain_ref[...] * (z * sigmoid(z))).astype(BF16)


def silu_slope(p, s):
    return s * (1.0 + p * (1.0 - s))


def grads_kernel(
    q_ref, k_ref, v_ref, z_ref, beta_ref, decay_ref, alog_ref, bias_ref, conv_ref, gain_ref, gh_ref,
    gq_ref, gk_ref, gv_ref, gz_ref, gbeta_ref, gdecay_ref, gconv_ref, galog_ref, gbias_ref, ggain_ref,
    dbeta_acc, ddecay_acc,
):
    size = q_ref.shape[0]
    rows, cols = grids(size)
    betas, logit, decay = gates(beta_ref, decay_ref, alog_ref, bias_ref)
    totals = running(decay, rows, cols)
    step = pl.program_id(0)
    first = step * STEP_HEADS

    @pl.when(step == 0)
    def _():
        dbeta_acc[...] = jnp.zeros_like(dbeta_acc)
        ddecay_acc[...] = jnp.zeros_like(ddecay_acc)
        ggain_ref[...] = jnp.zeros_like(ggain_ref)

    lanes = lax.broadcasted_iota(jnp.int32, betas.shape, 1)
    gain = gain_ref[...]
    dbeta_all = jnp.zeros(betas.shape, F32)
    dtotal_all = jnp.zeros(betas.shape, F32)
    dgain = jnp.zeros_like(gain)
    for i in range(STEP_HEADS):
        at = slice(i * DK, (i + 1) * DK)
        xs = (q_ref[:, at].astype(F32), k_ref[:, at].astype(F32), v_ref[:, at].astype(F32))
        ws = (conv_ref[0, :, at], conv_ref[1, :, at], conv_ref[2, :, at])
        beta = column(betas, first + i)
        mixed, saved = forward(*xs, *ws, beta, column(totals, first + i), rows, cols)
        ps, ss, value, (rq, rk), (query, key), (query_s, key_s) = saved[:6]
        weights, strict, key_dots, mixing, inverse, corrected = saved[6:]

        z = z_ref[:, at].astype(F32)
        sz = sigmoid(z)
        gh = gh_ref[:, at].astype(F32)
        r = lax.rsqrt(jnp.mean(mixed * mixed, axis=1, keepdims=True) + EPS)
        unit = mixed * r
        gz_ref[:, at] = (gh * unit * gain * silu_slope(z, sz)).astype(BF16)
        dnorm = gh * (z * sz)
        dgain = dgain + jnp.sum(dnorm * unit, axis=0, keepdims=True)
        dunit = dnorm * gain
        dmixed = r * (dunit - unit * jnp.mean(unit * dunit, axis=1, keepdims=True))

        dmixed_s = split(dmixed)
        corrected_s = split(corrected)
        dmixing = mm_t(dmixed_s, corrected_s)
        dcorrected = mm(split(mixing.T), dmixed_s)
        drhs = mm(split(inverse.T), split(dcorrected))
        dsystem = -mm_t(split(drhs), corrected_s)
        dvalue = beta * drhs
        swept = dsystem * strict * key_dots
        dbeta = jnp.sum(drhs * value, axis=1, keepdims=True) + jnp.sum(swept, axis=1, keepdims=True)
        flow = dmixing * mixing + beta * swept
        flow_cols = jnp.sum(flow, axis=0, keepdims=True)
        flow_col = jnp.sum(jnp.where(rows == cols, flow_cols, 0.0), axis=1, keepdims=True)
        dtotal = jnp.sum(flow, axis=1, keepdims=True) - flow_col
        ddots = dmixing * weights
        pair = beta * dsystem * strict
        dquery = mm(split(ddots), key_s) * DK**-0.5
        dkey = mm(split(ddots.T), query_s) + mm(split(pair + pair.T), key_s)

        here = lanes == first + i
        dbeta_all = dbeta_all + jnp.where(here, dbeta, 0.0)
        dtotal_all = dtotal_all + jnp.where(here, dtotal, 0.0)

        dyq = rq * (dquery - query * jnp.sum(query * dquery, axis=1, keepdims=True))
        dyk = rk * (dkey - key * jnp.sum(key * dkey, axis=1, keepdims=True))
        for kind, (dy, ref) in enumerate(((dyq, gq_ref), (dyk, gk_ref), (dvalue, gv_ref))):
            dp = dy * silu_slope(ps[kind], ss[kind])
            w = ws[kind]
            taps = w.shape[0]
            dx = w[taps - 1 : taps] * dp
            for j in range(taps - 1):
                dx = dx + w[j : j + 1] * shift_up(dp, taps - 1 - j)
            ref[:, at] = dx.astype(BF16)
            for j in range(taps):
                gconv_ref[kind, j : j + 1, at] = jnp.sum(
                    dp * shift_down(xs[kind], taps - 1 - j), axis=0, keepdims=True
                )

    upper = (rows <= cols).astype(F32)
    dbeta_acc[...] += dbeta_all
    ddecay_acc[...] += jnp.dot(
        upper, dtotal_all, precision=lax.Precision.HIGHEST, preferred_element_type=F32
    )
    ggain_ref[...] += dgain

    @pl.when(step == pl.num_programs(0) - 1)
    def _():
        gbeta_ref[...] = (dbeta_acc[...] * betas * (1.0 - betas)).astype(BF16)
        ddecay = ddecay_acc[...]
        dlogit = -jnp.exp(alog_ref[...]) * sigmoid(logit) * ddecay
        gdecay_ref[...] = dlogit.astype(BF16)
        galog_ref[...] = jnp.sum(ddecay * decay, axis=0, keepdims=True)
        gbias_ref[...] = jnp.sum(dlogit, axis=0, keepdims=True)


def specs(tokens, heads, taps):
    width = STEP_HEADS * DK
    wide = pl.BlockSpec((tokens, width), lambda i: (0, i))
    small = pl.BlockSpec((tokens, heads), lambda i: (0, 0))
    row = pl.BlockSpec((1, heads), lambda i: (0, 0))
    taps_spec = pl.BlockSpec((3, taps, width), lambda i: (0, 0, i))
    gain = pl.BlockSpec((1, DK), lambda i: (0, 0))
    return wide, small, row, taps_spec, gain


PARAMS = pltpu.CompilerParams(vmem_limit_bytes=48 * 2**20)


def run_hidden(q, k, v, z, beta, decay, alog, bias, conv_weight, gain):
    tokens, features = q.shape
    heads = beta.shape[1]
    wide, small, row, taps, gains = specs(tokens, heads, conv_weight.shape[1])
    return pl.pallas_call(
        hidden_kernel,
        grid=(heads // STEP_HEADS,),
        out_shape=jax.ShapeDtypeStruct((tokens, features), BF16),
        in_specs=[wide] * 4 + [small] * 2 + [row] * 2 + [taps, gains],
        out_specs=wide,
        compiler_params=PARAMS,
        cost_estimate=pl.CostEstimate(flops=2 * 10**10, bytes_accessed=4 * 10**6, transcendentals=0),
        name="hidden",
    )(q, k, v, z, beta, decay, alog, bias, conv_weight, gain)


def run_grads(q, k, v, z, beta, decay, alog, bias, conv_weight, gain, gh):
    tokens, features = q.shape
    heads = beta.shape[1]
    wide, small, row, taps, gains = specs(tokens, heads, conv_weight.shape[1])
    big = jax.ShapeDtypeStruct((tokens, features), BF16)
    little = jax.ShapeDtypeStruct((tokens, heads), BF16)
    line = jax.ShapeDtypeStruct((1, heads), F32)
    return pl.pallas_call(
        grads_kernel,
        grid=(heads // STEP_HEADS,),
        out_shape=[big] * 4 + [little] * 2
        + [jax.ShapeDtypeStruct(conv_weight.shape, F32), line, line, jax.ShapeDtypeStruct((1, DK), F32)],
        in_specs=[wide] * 4 + [small] * 2 + [row] * 2 + [taps, gains, wide],
        out_specs=[wide] * 4 + [small] * 2 + [taps, row, row, gains],
        scratch_shapes=[pltpu.VMEM((tokens, heads), F32), pltpu.VMEM((tokens, heads), F32)],
        compiler_params=PARAMS,
        cost_estimate=pl.CostEstimate(flops=4 * 10**10, bytes_accessed=8 * 10**6, transcendentals=0),
        name="grads",
    )(q, k, v, z, beta, decay, alog, bias, conv_weight, gain, gh)


def sum_rep(part, size):
    if size == 2:
        return part + lax.ppermute(part, "rep", [(0, 1), (1, 0)])
    return lax.psum(part, "rep")


def shards(
    reps, queries_in, keys_in, values_in, gate_z, beta_logit, decay_in, a_log, dt_bias,
    conv_weight, norm_gain, out_weight, out_grad,
):
    inputs = (
        queries_in, keys_in, values_in, gate_z, beta_logit, decay_in,
        a_log[None, :], dt_bias[None, :], conv_weight, norm_gain[None, :],
    )
    gathered = lax.all_gather(out_weight, "shard", axis=0, tiled=True)
    hidden = run_hidden(*inputs)
    hidden_all = lax.all_to_all(hidden, "shard", split_axis=1, concat_axis=0, tiled=True)
    grad_all = lax.all_gather(out_grad, "shard", axis=0, tiled=True)
    grad_hidden = lax.dot_general(
        out_grad, gathered, (((1,), (1,)), ((), ())), preferred_element_type=F32
    ).astype(BF16)
    grads = run_grads(*inputs, grad_hidden)
    layer_out = jnp.dot(hidden, gathered, preferred_element_type=F32).astype(BF16)
    packed = jnp.concatenate(
        [grads[6].reshape(-1), grads[7].reshape(-1), grads[8].reshape(-1), grads[9].reshape(-1)]
    )
    packed = lax.psum(packed, ("shard", "rep"))
    own = lax.dot_general(
        hidden_all, grad_all, (((0,), (0,)), ((), ())), preferred_element_type=F32
    )
    grad_out_weight = sum_rep(own, reps)
    n_conv, heads = conv_weight.size, a_log.shape[0]
    return (
        layer_out, grads[0], grads[1], grads[2], grads[3], grads[4], grads[5],
        packed[:n_conv].reshape(conv_weight.shape),
        packed[n_conv : n_conv + heads],
        packed[n_conv + heads : n_conv + 2 * heads],
        packed[n_conv + 2 * heads :],
        grad_out_weight,
    )


def solution(mesh):
    rows = P(("shard", "rep"), None)
    return jax.shard_map(
        functools.partial(shards, mesh.shape["rep"]),
        mesh=mesh,
        in_specs=(rows,) * 6 + (P(), P(), P(), P(), P("shard", None), rows),
        out_specs=(rows,) * 7 + (P(), P(), P(), P(), P("shard", None)),
        check_vma=False,
    )
```

time: 1050 us -> 523 us (0.50); the launches traced: 1040 us -> 523 us
  other arithmetic: 463 us -> 1.38 us
  Pallas kernels: 0 us -> 121 us
  matrix products: 120 us -> 22.5 us
  local copies, waits for them, and re-layouts: 86.3 us -> 16.4 us
  blocking collectives: 56.1 us -> 38.4 us
  waiting for transfers between devices: 295 us -> 308 us
    another operation x31 -> x0, other arithmetic: 412 us -> none  [the longest x18 403 us: advance(): jax.scipy.linalg.solve_triangular(system, rhs_side, lower=True, unit_diag...]
    reduce_scatter x1 -> x0, waiting for transfers between devices: 151 us -> none  [shards(): lax.psum_scatter(lax.dot_general(hidden, out_grad, (((0,), (0,)), ((), ()...]
    all_gather x1, waiting for transfers between devices: 0.01 us -> 148 us  [shards(): gathered = lax.all_gather(out_weight, 'shard', axis=0, tiled=True)]
    pallas_call x0 -> x2, Pallas kernels: none -> 121 us  [the longest x1 71.1 us: run_grads(): pl.pallas_call(grads_kernel, grid=(heads // STEP_HEADS,), out_shape=[big]...]
    dot_general x45 -> x3, matrix products: 105 us -> 22.5 us  [the longest x1 9.21 us: shards(): lax.dot_general(out_grad, gathered, (((1,), (1,)), ((), ())), preferred_e...]
    psum x1 -> x0, blocking collectives: 56.1 us -> none  [shards(): lax.psum((grads[6], grads[7], grads[8], grads[9]), ('shard', 'rep'))]
    all_gather x0 -> x1, waiting for transfers between devices: none -> 44.3 us  [shards(): grad_all = lax.all_gather(out_grad, 'shard', axis=0, tiled=True)]
    all_to_all x0 -> x1, blocking collectives: none -> 38.4 us  [shards(): lax.all_to_all(hidden, 'shard', split_axis=1, concat_axis=0, tiled=True)]
  transfers between devices with their start and end apart: 4 -> 4, of which waited for: 3 -> 4; matrix products, arithmetic and copies ran while one was open for 60% -> 3% of each run, Pallas kernels for 0% -> 10%
where the time goes in v1:
time: 523 us
  waiting for transfers between devices  308 us (59%)
  Pallas kernels  121 us (23%)
  blocking collectives  38.4 us (7%)
  matrix products  22.5 us (4%)
  local copies, waits for them, and re-layouts  16.4 us (3%)
  between operations  13.9 us (3%)
    all_gather x1, waiting for transfers between devices, shards(): gathered = lax.all_gather(out_weight, 'shard', axis=0, tiled=True)  148 us
    psum x1, waiting for transfers between devices, shards(): packed = lax.psum(packed, ('shard', 'rep'))  111 us
    pallas_call x1, Pallas kernels, run_grads(): pl.pallas_call(grads_kernel, grid=(heads // STEP_HEADS,), out_shape=[big]...  71.1 us
    pallas_call x1, Pallas kernels, run_hidden(): pl.pallas_call(hidden_kernel, grid=(heads // STEP_HEADS,), out_shape=jax....  50.1 us
    all_gather x1, waiting for transfers between devices, shards(): grad_all = lax.all_gather(out_grad, 'shard', axis=0, tiled=True)  44.3 us
    all_to_all x1, blocking collectives, shards(): lax.all_to_all(hidden, 'shard', split_axis=1, concat_axis=0, tiled=True)  38.4 us
    unnamed x36, local copies, waits for them, and re-layouts  11.2 us
  transfers between devices with their start and end apart: 4, of which 4 were waited for; matrix products, arithmetic and copies ran while one was open for 3% of the time, Pallas kernels for 10%

profile of v1, /device:TPU:0, one launch (start us, length us, event | category | flops | bytes accessed | tf_op | source)
XLA Modules:
  0.0 522.6 jit_solution(4296965800993348119)
XLA Ops:
  7.2 0.0 all-gather.5.cloned.1.call-start
  7.2 0.7 all-gather.5.cloned.1.call-update
  7.9 0.0 all-gather.3.cloned.1.call-start
  8.0 0.7 all-gather.3.cloned.1.call-update
  8.7 0.0 all-reduce.2.cloned.1.call-start
  8.7 0.8 copy.30.beta_ref
  9.5 0.8 copy.31.decay_ref
  10.3 1.1 copy-done
  11.4 1.1 copy-done.2
  12.5 1.1 copy-done.4
  13.6 1.1 copy-done.6
  14.7 0.9 copy-done.8
  15.6 0.7 copy-done.10
  16.3 0.7 copy-done.12
  16.9 0.7 copy-done.14
  17.6 50.1 %hidden.1 = bf16[128,2560]{1,0:T(8,128)(2,1)S(1)} custom-call(bf16[128,2560]{1,0:T(8,128)(2,1)S(1)} %copy-done, bf16[128,2560]{1,0:T(8,128)(2,1)S(1)} %copy-done.2, bf16[128,2560]{1,0:T(8,128)(2,1)S(1)} %copy-done.4, bf16[128,2560]{1,0:T(8,128)(2,1)S(1)} %copy-done.6, bf16[128,20]{1,0:T(8,128)(2,1)S(1)} %copy.30.beta_ref, ...), custom_call_target="tpu_custom_call" | custom-call | flops 20000000000 | bytes 4000000 | tf_op jit(solution)/shard_map/hidden/pallas_call | solution.py:267
  67.7 0.3 copy.34
  68.0 38.4 %all_to_all.19 = bf16[128,16,160]{0,2,1:T(8,128)(2,1)S(1)} all-to-all(bf16[128,16,160]{0,2,1:T(8,128)(2,1)S(1)} %bitcast.29), channel_id=1, replica_groups=mesh['shard'=16,'rep'=2] {'shard'}, dimensions={1} | all-to-all | bytes 1310720 | tf_op jit(solution)/shard_map/all_to_all | solution.py:316
  106.4 44.3 %all-gather.5.cloned.1.call-done = bf16[2048,2560]{1,0:T(8,128)(2,1)} async-done(((bf16[128,2560]{1,0:T(8,128)(2,1)}), bf16[2048,2560]{1,0:T(8,128)(2,1)}) %all-gather.5.cloned.1.call-update) | async-done | bytes 10485776 | tf_op jit(solution)/shard_map/all_gather | solution.py:317
  150.7 5.8 %fusion = f32[160,2560]{1,0:T(8,128)S(1)} fusion(bf16[2048,2560]{1,0:T(8,128)(2,1)} %all-gather.5.cloned.1.call-done, bf16[128,16,160]{0,2,1:T(8,128)(2,1)S(1)} %all_to_all.19), kind=kOutput, calls=%fused_computation.2 | convolution fusion | flops 1677721600 | bytes 12779520 | tf_op jit(solution)/shard_map/dot_general | solution.py:327
  156.5 0.0 copy-start.1
  156.6 0.0 copy-start.3
  156.6 0.0 copy-start.5
  156.6 0.0 copy-start.7
  156.6 0.0 copy-start.11
  156.6 0.0 copy-start.13
  156.6 0.0 copy-start.15
  156.6 0.1 collective-permute-start
  156.7 3.5 collective-permute-done
  160.2 1.4 add.5
  161.6 148.0 %all-gather.3.cloned.1.call-done = bf16[2560,2560]{1,0:T(8,128)(2,1)} async-done(((bf16[160,2560]{1,0:T(8,128)(2,1)}), bf16[2560,2560]{1,0:T(8,128)(2,1)}) %all-gather.3.cloned.1.call-update) | async-done | bytes 13107216 | tf_op jit(solution)/shard_map/all_gather | solution.py:314
  309.6 9.2 %convolution_convert_fusion.gh_ref = bf16[128,2560]{1,0:T(8,128)(2,1)S(1)} fusion(bf16[128,2560]{1,0:T(8,128)(2,1)} %param.23, bf16[2560,2560]{1,0:T(8,128)(2,1)} %all-gather.3.cloned.1.call-done), kind=kOutput, calls=%fused_computation | convolution fusion | flops 1678049280 | bytes 14417920 | tf_op jit(solution)/shard_map/dot_general | solution.py:318
  318.8 0.0 copy-done.1
  318.8 0.0 copy-done.3
  318.8 0.0 copy-done.5
  318.8 0.0 copy-start.9
  318.9 0.9 copy-done.9
  319.8 71.1 %grads.1 = (bf16[128,2560]{1,0:T(8,128)(2,1)}, bf16[128,2560]{1,0:T(8,128)(2,1)}, bf16[128,2560]{1,0:T(8,128)(2,1)}, bf16[128,2560]{1,0:T(8,128)(2,1)}, bf16[128...) custom-call(bf16[128,2560]{1,0:T(8,128)(2,1)S(1)} %copy-done.1, ...), custom_call_target="tpu_custom_call" | custom-call | flops 40000000000 | bytes 8000000 | tf_op jit(solution)/shard_map/grads/pallas_call | solution.py:286
  390.9 0.7 concatenate.3
  391.6 0.0 all-reduce.2.cloned.1.call-update
  391.6 7.5 %convolution_convert_fusion.1 = bf16[128,2560]{1,0:T(8,128)(2,1)} fusion(bf16[128,2560]{1,0:T(8,128)(2,1)S(1)} %hidden.1, bf16[2560,2560]{1,0:T(8,128)(2,1)} %all-gather.3.cloned.1.call-done), kind=kOutput, calls=%fused_computation.1 | convolution fusion | flops 1678049280 | bytes 14417920 | tf_op jit(solution)/shard_map/dot_general | solution.py:322
  399.1 0.7 copy.36
  399.8 0.7 copy.37
  400.5 111.4 %all-reduce.2.cloned.1.call-done = f32[30888]{0:T(1024)} async-done(((f32[30888]{0:T(1024)}), f32[30888]{0:T(1024)}) %all-reduce.2.cloned.1.call-update) | async-done | bytes 123568 | tf_op jit(solution)/shard_map/psum | solution.py:326
  511.8 0.9 slice.16
  512.7 0.7 reshape.46
  513.4 1.3 fusion.3
  514.8 1.3 slice.19
  (13 shorter events, 0.1 us)
Async XLA Ops:
  7.2 143.5 %all-gather.5.cloned.1.call-start = ((), (), s32[]{:S(2)}) async-start(), calls=%async_computation.3 | async-start | bytes 11141120 | tf_op jit(solution)/shard_map/all_gather | solution.py:317
  7.9 301.6 %all-gather.3.cloned.1.call-start = ((), (), s32[]{:S(2)}) async-start(), calls=%async_computation.1 | async-start | bytes 13926400 | tf_op jit(solution)/shard_map/all_gather | solution.py:314
  8.7 503.2 %all-reduce.2.cloned.1.call-start = ((), (), s32[]{:S(2)}) async-start(), calls=%async_computation.2 | async-start | bytes 253952 | tf_op jit(solution)/shard_map/psum | solution.py:326
  10.3 1.1 copy-start
  11.4 1.1 copy-start.2
  12.5 1.1 copy-start.4
  13.6 1.1 copy-start.6
  14.7 0.9 copy-start.8
  15.6 0.7 copy-start.10
  16.3 0.7 copy-start.12
  16.9 0.7 copy-start.14
  156.5 162.2 %copy-start.1 = (bf16[128,2560]{1,0:T(8,128)(2,1)S(1)}, bf16[128,2560]{1,0:T(8,128)(2,1)}, u32[]{:S(2)}) copy-start(bf16[128,2560]{1,0:T(8,128)(2,1)} %q_ref.3) | copy-start | bytes 1966084
  156.6 162.2 %copy-start.3 = (bf16[128,2560]{1,0:T(8,128)(2,1)S(1)}, bf16[128,2560]{1,0:T(8,128)(2,1)}, u32[]{:S(2)}) copy-start(bf16[128,2560]{1,0:T(8,128)(2,1)} %k_ref.3) | copy-start | bytes 1966084
  156.6 162.2 %copy-start.5 = (bf16[128,2560]{1,0:T(8,128)(2,1)S(1)}, bf16[128,2560]{1,0:T(8,128)(2,1)}, u32[]{:S(2)}) copy-start(bf16[128,2560]{1,0:T(8,128)(2,1)} %v_ref.3) | copy-start | bytes 1966084
  156.6 162.2 %copy-start.7 = (bf16[128,2560]{1,0:T(8,128)(2,1)S(1)}, bf16[128,2560]{1,0:T(8,128)(2,1)}, u32[]{:S(2)}) copy-start(bf16[128,2560]{1,0:T(8,128)(2,1)} %z_ref.3) | copy-start | bytes 1966084
  156.6 162.2 %copy-start.11 = (f32[20]{0:T(128)S(1)}, f32[20]{0:T(128)}, u32[]{:S(2)}) copy-start(f32[20]{0:T(128)} %param.18) | copy-start | bytes 244
  156.6 162.2 %copy-start.13 = (f32[20]{0:T(128)S(1)}, f32[20]{0:T(128)}, u32[]{:S(2)}) copy-start(f32[20]{0:T(128)} %param.19) | copy-start | bytes 244
  156.6 162.2 %copy-start.15 = (f32[128]{0:T(128)S(1)}, f32[128]{0:T(128)}, u32[]{:S(2)}) copy-start(f32[128]{0:T(128)} %param.21) | copy-start | bytes 1540
  156.6 3.6 collective-permute-start
  318.8 0.9 copy-start.9
Sparse Core Ops, SparseCore 0:
  10.7 139.9 all-gather.4
  153.5 156.0 all-gather.2
  391.8 120.0 all-reduce.1

commit v2 on v1

--- a/solution.py
+++ b/solution.py
@@ -271,7 +271,7 @@
         in_specs=[wide] * 4 + [small] * 2 + [row] * 2 + [taps, gains],
         out_specs=wide,
         compiler_params=PARAMS,
-        cost_estimate=pl.CostEstimate(flops=2 * 10**10, bytes_accessed=4 * 10**6, transcendentals=0),
+        cost_estimate=pl.CostEstimate(flops=6 * 10**10, bytes_accessed=4 * 10**6, transcendentals=0),
         name="hidden",
     )(q, k, v, z, beta, decay, alog, bias, conv_weight, gain)
 
@@ -292,9 +292,60 @@
         out_specs=[wide] * 4 + [small] * 2 + [taps, row, row, gains],
         scratch_shapes=[pltpu.VMEM((tokens, heads), F32), pltpu.VMEM((tokens, heads), F32)],
         compiler_params=PARAMS,
-        cost_estimate=pl.CostEstimate(flops=4 * 10**10, bytes_accessed=8 * 10**6, transcendentals=0),
+        cost_estimate=pl.CostEstimate(flops=8 * 10**10, bytes_accessed=8 * 10**6, transcendentals=0),
         name="grads",
     )(q, k, v, z, beta, decay, alog, bias, conv_weight, gain, gh)
+
+
+def total_kernel(sizes, x_ref, out_ref, arrived, send_sem, recv_sem):
+    names = tuple(sizes)
+    where = {name: lax.axis_index(name) for name in names}
+    partners = []
+    for name in reversed(names):
+        bit = 1
+        while bit < sizes[name]:
+            me = where[name]
+            other = me + bit * (1 - 2 * lax.rem(me // bit, 2))
+            partners.append(tuple(other if n == name else where[n] for n in names))
+            bit *= 2
+    barrier = pltpu.get_barrier_semaphore()
+    for partner in partners:
+        pl.semaphore_signal(barrier, inc=1, device_id=partner, device_id_type=pl.DeviceIdType.MESH)
+    pl.semaphore_wait(barrier, len(partners))
+    out_ref[...] = x_ref[...]
+    for i, partner in enumerate(partners):
+        copy = pltpu.make_async_remote_copy(
+            src_ref=out_ref,
+            dst_ref=arrived.at[i],
+            send_sem=send_sem.at[i],
+            recv_sem=recv_sem.at[i],
+            device_id=partner,
+            device_id_type=pl.DeviceIdType.MESH,
+        )
+        copy.start()
+        copy.wait()
+        out_ref[...] += arrived[i]
+
+
+def run_total(x, sizes):
+    rounds = sum(size.bit_length() - 1 for size in sizes.values())
+    vmem = pl.BlockSpec(memory_space=pltpu.VMEM)
+    return pl.pallas_call(
+        functools.partial(total_kernel, sizes),
+        out_shape=jax.ShapeDtypeStruct(x.shape, x.dtype),
+        in_specs=[vmem],
+        out_specs=vmem,
+        scratch_shapes=[
+            pltpu.VMEM((rounds, *x.shape), x.dtype),
+            pltpu.SemaphoreType.DMA((rounds,)),
+            pltpu.SemaphoreType.DMA((rounds,)),
+        ],
+        compiler_params=pltpu.CompilerParams(
+            collective_id=0, has_side_effects=True, vmem_limit_bytes=16 * 2**20
+        ),
+        cost_estimate=pl.CostEstimate(flops=10**10, bytes_accessed=30 * 10**6, transcendentals=0),
+        name="total",
+    )(x)
 
 
 def sum_rep(part, size):
@@ -304,37 +355,63 @@
 
 
 def shards(
-    reps, queries_in, keys_in, values_in, gate_z, beta_logit, decay_in, a_log, dt_bias,
+    sizes, queries_in, keys_in, values_in, gate_z, beta_logit, decay_in, a_log, dt_bias,
     conv_weight, norm_gain, out_weight, out_grad,
 ):
     inputs = (
         queries_in, keys_in, values_in, gate_z, beta_logit, decay_in,
         a_log[None, :], dt_bias[None, :], conv_weight, norm_gain[None, :],
     )
-    gathered = lax.all_gather(out_weight, "shard", axis=0, tiled=True)
+    reps = sizes["rep"]
+    rep = lax.axis_index("rep")
+    share = out_weight.shape[1] // reps
+    mine = lax.all_gather(
+        lax.dynamic_slice_in_dim(out_weight, rep * share, share, axis=1), "shard", axis=0, tiled=True
+    )
     hidden = run_hidden(*inputs)
+    out_grad_late, mine, hidden = lax.optimization_barrier((out_grad, mine, hidden))
     hidden_all = lax.all_to_all(hidden, "shard", split_axis=1, concat_axis=0, tiled=True)
-    grad_all = lax.all_gather(out_grad, "shard", axis=0, tiled=True)
-    grad_hidden = lax.dot_general(
-        out_grad, gathered, (((1,), (1,)), ((), ())), preferred_element_type=F32
+    grad_all = lax.all_gather(out_grad_late, "shard", axis=0, tiled=True)
+    parts = [mine] + [
+        lax.ppermute(mine, "rep", [((i + k) % reps, i) for i in range(reps)]) for k in range(1, reps)
+    ]
+    back_dims = (((1,), (1,)), ((), ()))
+    grad_hidden = sum(
+        lax.dot_general(
+            lax.dynamic_slice_in_dim(out_grad, lax.rem(rep + k, reps) * share, share, axis=1),
+            part, back_dims, preferred_element_type=F32,
+        )
+        for k, part in enumerate(parts)
     ).astype(BF16)
     grads = run_grads(*inputs, grad_hidden)
-    layer_out = jnp.dot(hidden, gathered, preferred_element_type=F32).astype(BF16)
-    packed = jnp.concatenate(
-        [grads[6].reshape(-1), grads[7].reshape(-1), grads[8].reshape(-1), grads[9].reshape(-1)]
-    )
-    packed = lax.psum(packed, ("shard", "rep"))
+    pieces = jnp.stack(
+        [jnp.dot(hidden, part, preferred_element_type=F32).astype(BF16) for part in parts]
+    )
+    layer_out = jnp.concatenate(
+        [
+            lax.dynamic_index_in_dim(pieces, lax.rem(i - rep + reps, reps), 0, keepdims=False)
+            for i in range(reps)
+        ],
+        axis=1,
+    )
+    small = jnp.concatenate([grads[i].reshape(-1) for i in range(6, 10)])
+    filled = -small.size % (8 * 128)
+    packed = run_total(jnp.pad(small, (0, filled)).reshape(-1, 128), sizes).reshape(-1)
+    hidden_all, grad_all, packed, layer_out = lax.optimization_barrier(
+        (hidden_all, grad_all, packed, layer_out)
+    )
     own = lax.dot_general(
         hidden_all, grad_all, (((0,), (0,)), ((), ())), preferred_element_type=F32
     )
     grad_out_weight = sum_rep(own, reps)
     n_conv, heads = conv_weight.size, a_log.shape[0]
+    gain_at = n_conv + 2 * heads
     return (
         layer_out, grads[0], grads[1], grads[2], grads[3], grads[4], grads[5],
         packed[:n_conv].reshape(conv_weight.shape),
         packed[n_conv : n_conv + heads],
-        packed[n_conv + heads : n_conv + 2 * heads],
-        packed[n_conv + 2 * heads :],
+        packed[n_conv + heads : gain_at],
+        packed[gain_at : gain_at + norm_gain.size],
         grad_out_weight,
     )
 
@@ -342,7 +419,7 @@
 def solution(mesh):
     rows = P(("shard", "rep"), None)
     return jax.shard_map(
-        functools.partial(shards, mesh.shape["rep"]),
+        functools.partial(shards, dict(mesh.shape)),
         mesh=mesh,
         in_specs=(rows,) * 6 + (P(), P(), P(), P(), P("shard", None), rows),
         out_specs=(rows,) * 7 + (P(), P(), P(), P(), P("shard", None)),

time: 523 us -> 281 us (0.54)
  waiting for transfers between devices: 308 us -> 60.2 us
  blocking collectives: 38.4 us -> 0 us
  Pallas kernels: 121 us -> 157 us
    all_gather x2, waiting for transfers between devices: 192 us -> 43 us  [the longest x1 43 us: shards(): lax.all_gather(lax.dynamic_slice_in_dim(out_weight, rep * share, share, a...]
    psum x1 -> x0, waiting for transfers between devices: 111 us -> none  [shards(): packed = lax.psum(packed, ('shard', 'rep'))]
    all_to_all x1 -> x0, blocking collectives: 38.4 us -> none  [shards(): lax.all_to_all(hidden, 'shard', split_axis=1, concat_axis=0, tiled=True)]
    pallas_call x0 -> x1, Pallas kernels: none -> 36.1 us  [run_total(): pl.pallas_call(functools.partial(total_kernel, sizes), out_shape=jax.Shap...]
    all_to_all x0 -> x1, waiting for transfers between devices: none -> 16.8 us  [shards(): lax.all_to_all(hidden, 'shard', split_axis=1, concat_axis=0, tiled=True)]
    unnamed x36 -> x42, local copies, waits for them, and re-layouts: 11.2 us -> 11.4 us
    dot_general x2 -> x4, matrix products: 16.7 us -> 16.7 us  [the longest x2 11.8 us: shards(): lax.dot_general(lax.dynamic_slice_in_dim(out_grad, lax.rem(rep + k, reps)...]
  transfers between devices with their start and end apart: 4 -> 5, of which waited for: 4 -> 3; matrix products, arithmetic and copies ran while one was open for 3% -> 9% of each run, Pallas kernels for 10% -> 56%
where the time goes in v2:
time: 281 us; the launch traced here: 280 us
  Pallas kernels  157 us (56%)
  waiting for transfers between devices  60.2 us (21%)
  matrix products  22.8 us (8%)
  local copies, waits for them, and re-layouts  17.3 us (6%)
  between operations  14.3 us (5%)
  starting transfers between devices  4.67 us (2%)
  other arithmetic  3.9 us (1%)
    pallas_call x1, Pallas kernels, run_grads(): pl.pallas_call(grads_kernel, grid=(heads // STEP_HEADS,), out_shape=[big]...  71.1 us
    pallas_call x1, Pallas kernels, run_hidden(): pl.pallas_call(hidden_kernel, grid=(heads // STEP_HEADS,), out_shape=jax....  50.1 us
    all_gather x1, waiting for transfers between devices, shards(): lax.all_gather(lax.dynamic_slice_in_dim(out_weight, rep * share, share, a...  43 us
    pallas_call x1, Pallas kernels, run_total(): pl.pallas_call(functools.partial(total_kernel, sizes), out_shape=jax.Shap...  36.1 us
    all_to_all x1, waiting for transfers between devices, shards(): lax.all_to_all(hidden, 'shard', split_axis=1, concat_axis=0, tiled=True)  16.8 us
    dot_general x2, matrix products, shards(): lax.dot_general(lax.dynamic_slice_in_dim(out_grad, lax.rem(rep + k, reps)...  11.8 us
    unnamed x42, local copies, waits for them, and re-layouts  11.4 us
    dot_general x1, matrix products, shards(): lax.dot_general(hidden_all, grad_all, (((0,), (0,)), ((), ())), preferred...  6.06 us
  transfers between devices with their start and end apart: 5, of which 3 were waited for; matrix products, arithmetic and copies ran while one was open for 9% of the time, Pallas kernels for 56%

profile of v2, /device:TPU:0, one launch (start us, length us, event | category | flops | bytes accessed | tf_op | source)
XLA Modules:
  0.0 280.4 jit_solution(1095063640444727893)
XLA Ops:
  7.2 0.0 copy-start
  7.2 0.0 all-gather.3.cloned.1.call-start
  7.2 1.1 copy-done
  8.3 0.8 constant_dynamic-slice_fusion
  9.1 0.0 all-gather.3.cloned.1.call-update
  9.1 0.0 all-gather.5.cloned.1.call-start
  9.2 0.8 copy.30.beta_ref
  10.0 0.8 copy.31.decay_ref
  10.8 1.1 copy-done.1
  11.9 1.1 copy-done.3
  13.0 1.1 copy-done.5
  14.1 1.1 copy-done.7
  15.2 0.9 copy-done.9
  16.1 0.7 copy-done.11
  16.7 0.7 copy-done.13
  17.4 0.7 copy-done.15
  18.0 50.1 %hidden.1 = bf16[128,2560]{1,0:T(8,128)(2,1)S(1)} custom-call(bf16[128,2560]{1,0:T(8,128)(2,1)S(1)} %copy-done.1, bf16[128,2560]{1,0:T(8,128)(2,1)S(1)} %copy-done.3, bf16[128,2560]{1,0:T(8,128)(2,1)S(1)} %copy-done.5, bf16[128,2560]{1,0:T(8,128)(2,1)S(1)} %copy-done.7, bf16[128,20]{1,0:T(8,128)(2,1)S(1)} %copy.30.beta_ref, ...), custom_call_target="tpu_custom_call" | custom-call | flops 60000002048 | bytes 4000000 | tf_op jit(solution)/shard_map/hidden/pallas_call | solution.py:267
  68.1 43.0 %all-gather.3.cloned.1.call-done = bf16[2560,1280]{1,0:T(8,128)(2,1)} async-done(((bf16[160,1280]{1,0:T(8,128)(2,1)}), bf16[2560,1280]{1,0:T(8,128)(2,1)}) %all-gather.3.cloned.1.call-update) | async-done | bytes 6553616 | tf_op jit(solution)/shard_map/all_gather | solution.py:368
  111.1 0.0 all-gather.5.cloned.1.call-update
  111.1 0.1 collective-permute-start
  111.2 1.1 copy.32
  112.3 4.4 %all-to-all-start = ((bf16[128,16,160]{0,2,1:T(8,128)(2,1)}), bf16[128,16,160]{0,2,1:T(8,128)(2,1)}, u32[]{:S(2)}, u32[]{:S(2)}) async-start(bf16[128,16,160]{0,2,1:T(8,128)(2,1)} %bitcast.3), calls=%async_computation | async-start | bytes 1310720 | tf_op jit(solution)/shard_map/all_to_all | solution.py:373
  116.8 6.3 %fusion.8 = f32[128,2560]{1,0:T(8,128)} fusion(bf16[2560,1280]{1,0:T(8,128)(2,1)} %all-gather.3.cloned.1.call-done, bf16[128,2560]{1,0:T(8,128)(2,1)S(1)} %copy-done.18, s32[]{:T(128)S(6)} %select_n.17), kind=kOutput, calls=%fused_computation.17 | convolution fusion | flops 838860800 | bytes 8192004 | tf_op jit(solution)/shard_map/dot_general | solution.py:380
  123.1 1.0 fusion.1
  124.1 0.0 copy-start.2
  124.1 0.0 copy-start.4
  124.1 0.0 copy-start.10
  124.1 0.0 copy-start.12
  124.2 0.0 copy-start.16
  124.2 16.8 %all-to-all-done = bf16[128,16,160]{0,2,1:T(8,128)(2,1)} async-done(((bf16[128,16,160]{0,2,1:T(8,128)(2,1)}), bf16[128,16,160]{0,2,1:T(8,128)(2,1)}, u32[]{:S(2)}, u32[]{:S(2)}) %all-to-all-start) | async-done | bytes 655392 | tf_op jit(solution)/shard_map/all_to_all | solution.py:373
  141.0 2.1 copy_bitcast_fusion
  143.1 5.5 %fusion.gh_ref = bf16[128,2560]{1,0:T(8,128)(2,1)S(1)} fusion(f32[128,2560]{1,0:T(8,128)} %fusion.8, bf16[2560,1280]{1,0:T(8,128)(2,1)} %collective-permute-done, bf16[128,2560]{1,0:T(8,128)(2,1)} %param.23, s32[]{:T(128)S(6)} %select_n.18), kind=kOutput, calls=%fused_computation.1 | convolution fusion | flops 839516160 | bytes 8847364 | tf_op jit(solution)/shard_map/dot_general | solution.py:380
  148.7 71.1 %grads.1 = (bf16[128,2560]{1,0:T(8,128)(2,1)}, bf16[128,2560]{1,0:T(8,128)(2,1)}, bf16[128,2560]{1,0:T(8,128)(2,1)}, bf16[128,2560]{1,0:T(8,128)(2,1)}, bf16[128...) custom-call(bf16[128,2560]{1,0:T(8,128)(2,1)S(1)} %copy-done.2, ...), custom_call_target="tpu_custom_call" | custom-call | flops 80000000000 | bytes 8000000 | tf_op jit(solution)/shard_map/grads/pallas_call | solution.py:286
  219.8 0.1 concatenate.6
  219.9 3.9 %fusion.2 = bf16[1,128,1280]{2,1,0:T(8,128)(2,1)S(1)} fusion(bf16[128,2560]{1,0:T(8,128)(2,1)S(1)} %hidden.1, bf16[2560,1280]{1,0:T(8,128)(2,1)} %collective-permute-done), kind=kOutput, calls=%fused_computation.5 | convolution fusion | flops 839024640 | bytes 7536640 | tf_op jit(solution)/shard_map/dot_general | solution.py:388
  223.8 0.3 fusion.6
  224.1 0.9 pad_maximum_fusion
  225.0 36.1 %total.1 = f32[248,128]{1,0:T(8,128)S(1)} custom-call(f32[248,128]{1,0:T(8,128)S(1)} %pad_bitcast_fusion.x_ref), custom_call_target="tpu_custom_call" | custom-call | flops 10000000000 | bytes 30000000 | tf_op jit(solution)/shard_map/total/pallas_call | solution.py:333
  261.0 0.0 all-gather.5.cloned.1.call-done
  261.1 6.1 %fusion.13 = f32[160,2560]{1,0:T(8,128)S(1)} fusion(bf16[2048,160]{0,1:T(8,128)(2,1)} %copy_bitcast_fusion, bf16[2048,2560]{1,0:T(8,128)(2,1)} %all-gather.5.cloned.1.call-done), kind=kOutput, calls=%fused_computation.24 | convolution fusion | flops 1677721600 | bytes 12779520 | tf_op jit(solution)/shard_map/dot_general | solution.py:403
  267.1 0.1 collective-permute-start.1
  267.2 0.7 copy.36
  267.9 0.7 copy.37
  268.6 0.6 slice.15
  269.2 0.7 reshape.54
  269.9 0.6 fusion.12
  270.5 0.4 collective-permute-done.1
  270.8 2.8 add.44
  (27 shorter events, 0.1 us)
Async XLA Ops:
  7.2 1.2 copy-start
  7.2 103.9 %all-gather.3.cloned.1.call-start = ((), (), s32[]{:S(2)}) async-start(), calls=%async_computation.1 | async-start | bytes 6963200 | tf_op jit(solution)/shard_map/all_gather | solution.py:368
  9.1 251.9 %all-gather.5.cloned.1.call-start = ((), (), s32[]{:S(2)}) async-start(), calls=%async_computation.2 | async-start | bytes 11141120 | tf_op jit(solution)/shard_map/all_gather | solution.py:374
  10.8 1.1 copy-start.1
  11.9 1.1 copy-start.3
  13.0 1.1 copy-start.5
  14.1 1.1 copy-start.7
  15.2 0.9 copy-start.9
  16.1 0.7 copy-start.11
  16.7 0.7 copy-start.13
  17.4 0.7 copy-start.15
  18.0 98.7 %copy-start.18 = (bf16[128,2560]{1,0:T(8,128)(2,1)S(1)}, bf16[128,2560]{1,0:T(8,128)(2,1)}, u32[]{:S(2)}) copy-start(bf16[128,2560]{1,0:T(8,128)(2,1)} %param.23) | copy-start | bytes 1966084
  111.1 31.9 %collective-permute-start = (bf16[2560,1280]{1,0:T(8,128)(2,1)}, bf16[2560,1280]{1,0:T(8,128)(2,1)}, u32[]{:S(2)}, u32[]{:S(2)}) collective-permute-start(bf16[2560,1280]{1,0:T(8,128)(2,1)} %all-gather.3.cloned.1.call-done), channel_id=1, source_target_pairs={{1,0},{0,1},{3,2},{2,3},{5,4},{4,5},{7,6},{6,7},{9,8},{8,9},{11,10... | collective-permute-start | bytes 19660808 | tf_op jit(solution)/shard_map/ppermute | solution.py:376
  112.3 28.7 %all-to-all-start = ((bf16[128,16,160]{0,2,1:T(8,128)(2,1)}), bf16[128,16,160]{0,2,1:T(8,128)(2,1)}, u32[]{:S(2)}, u32[]{:S(2)}) async-start(bf16[128,16,160]{0,2,1:T(8,128)(2,1)} %bitcast.3), calls=%async_computation | async-start | bytes 1310720 | tf_op jit(solution)/shard_map/all_to_all | solution.py:373
  116.8 6.3 %copy-start.17 = (bf16[2560,1280]{1,0:T(8,128)(2,1)S(1)}, bf16[2560,1280]{1,0:T(8,128)(2,1)}, u32[]{:S(2)}) copy-start(bf16[2560,1280]{1,0:T(8,128)(2,1)} %all-gather.3.cloned.1.call-done) | copy-start | bytes 19660804
  124.1 24.5 %copy-start.2 = (bf16[128,2560]{1,0:T(8,128)(2,1)S(1)}, bf16[128,2560]{1,0:T(8,128)(2,1)}, u32[]{:S(2)}) copy-start(bf16[128,2560]{1,0:T(8,128)(2,1)} %q_ref.3) | copy-start | bytes 1966084
  124.1 24.5 %copy-start.4 = (bf16[128,2560]{1,0:T(8,128)(2,1)S(1)}, bf16[128,2560]{1,0:T(8,128)(2,1)}, u32[]{:S(2)}) copy-start(bf16[128,2560]{1,0:T(8,128)(2,1)} %k_ref.3) | copy-start | bytes 1966084
  124.1 24.5 %copy-start.10 = (f32[3,4,2560]{2,1,0:T(4,128)S(1)}, f32[3,4,2560]{2,1,0:T(4,128)}, u32[]{:S(2)}) copy-start(f32[3,4,2560]{2,1,0:T(4,128)} %conv_ref.3) | copy-start | bytes 368644
  124.1 24.5 %copy-start.12 = (f32[20]{0:T(128)S(1)}, f32[20]{0:T(128)}, u32[]{:S(2)}) copy-start(f32[20]{0:T(128)} %param.18) | copy-start | bytes 244
  124.2 24.5 %copy-start.14 = (f32[20]{0:T(128)S(1)}, f32[20]{0:T(128)}, u32[]{:S(2)}) copy-start(f32[20]{0:T(128)} %param.19) | copy-start | bytes 244
  124.2 24.5 %copy-start.16 = (f32[128]{0:T(128)S(1)}, f32[128]{0:T(128)}, u32[]{:S(2)}) copy-start(f32[128]{0:T(128)} %param.21) | copy-start | bytes 1540
  141.0 7.7 %copy-start.6 = (bf16[128,2560]{1,0:T(8,128)(2,1)S(1)}, bf16[128,2560]{1,0:T(8,128)(2,1)}, u32[]{:S(2)}) copy-start(bf16[128,2560]{1,0:T(8,128)(2,1)} %v_ref.3) | copy-start | bytes 1966084
  141.0 7.7 %copy-start.8 = (bf16[128,2560]{1,0:T(8,128)(2,1)S(1)}, bf16[128,2560]{1,0:T(8,128)(2,1)}, u32[]{:S(2)}) copy-start(bf16[128,2560]{1,0:T(8,128)(2,1)} %z_ref.3) | copy-start | bytes 1966084
  267.1 3.7 %collective-permute-start.1 = (f32[160,2560]{1,0:T(8,128)S(1)}, f32[160,2560]{1,0:T(8,128)}, u32[]{:S(2)}, u32[]{:S(2)}) collective-permute-start(f32[160,2560]{1,0:T(8,128)S(1)} %fusion.13), channel_id=1, source_target_pairs={{0,1},{1,0},{2,3},{3,2},{4,5},{5,4},{6,7},{7,6},{8,9},{9,8},{10,11... | collective-permute-start | bytes 4915208 | tf_op jit(solution)/shard_map/ppermute | solution.py:353
Sparse Core Ops, SparseCore 0:
  11.3 99.7 all-gather.2
  113.8 141.8 all-gather.4
